TPU v7x, 32 devices: a whole 2x2x4 slice. The times are simulated.
32 devices in a mesh: mp: 8 (over z, x), seq: 4 (over y, core).
Axes of the slice: x: 2, y: 2, z: 4, core: 2. Of those that a mesh axis runs over, the one named last changes fastest.
Arguments:
- hidden_in: bfloat16 [256, 8192], P(None, 'mp'), may hold values from -4 to 4
- attn_gain: bfloat16 [8192], P('mp'), may hold values from 0.099609375 to 1.8984375
- mlp_gain: bfloat16 [8192], replicated, may hold values from 0.099609375 to 1.8984375
- w_query: bfloat16 [8192, 8192], P('mp', 'seq'), may hold values from -1 to 1
- w_key: bfloat16 [8192, 1024], P('mp', 'seq'), may hold values from -1 to 1
- w_value: bfloat16 [8192, 1024], P('mp', 'seq'), may hold values from -0.0625 to 0.0625
- w_out: bfloat16 [8192, 8192], P('seq', 'mp'), may hold values from -0.0625 to 0.0625
- w_gate: bfloat16 [8192, 28672], P(None, ('mp', 'seq')), may hold values from -0.0625 to 0.0625
- w_up: bfloat16 [8192, 28672], P(None, ('mp', 'seq')), may hold values from -0.0625 to 0.0625
- w_down: bfloat16 [28672, 8192], P(('mp', 'seq')), may hold values from -0.03125 to 0.03125
- prompt_cache: bfloat16 [8, 8, 32768, 256], P(None, 'seq', 'mp'), may hold values from -136 to 136
- tail_cache: bfloat16 [128, 8, 512, 256], P('mp', 'seq'), may hold values from -136 to 136
- prompt_len: int32 [8], replicated, may hold values from 4096 to 32768, as said below
- tail_len: int32 [128], replicated, may hold values from 1 to 512, as said below
- prompt_of: int32 [128], replicated, may hold values from 0 to 7, as said below
Outputs:
- layer_out: bfloat16 [256, 8192], P(('mp', 'seq'))
- input_rms: float32 [256], replicated
- max_logit: float32 [128, 64], P(None, 'seq')
- new_entries: bfloat16 [128, 8, 2, 256], P('mp', 'seq')
Inputs may be any that keep to these rules, and one draw needn't show every extreme that they name: `prompt_len`: at least one prompt has 32768 positions. `tail_len`: at least one request has 512 tail positions. `prompt_of`: each prompt feeds exactly 16 requests.
All inputs are finite; a program needn't handle non-finite values.
Results may differ from a plain program's by a relative error of at most 0.028.
The roundings to bfloat16 on the way count: a program that leaves them out, or rounds other values in their place, can miss the bound.
Values may be sent and summed in bfloat16 or wider, within the bound.
A program may use at most 320 MiB of HBM per device.

v0:
```python
import jax
import jax.numpy as jnp
from jax import lax
from jax.sharding import PartitionSpec as P

D = 8192
HD = 128
PROMPTS = 8
CONT = 16
QPK = 8
REQ = 128
EPS = 1e-05
THETA = 500000.0
NEG = -1e30


def joined(part, axis, combine):
    gathered = jax.tree.map(lambda a: lax.all_gather(a, axis), part)

    def take(source):
        return jax.tree.map(lambda a: lax.dynamic_index_in_dim(a, source, 0, False), gathered)

    return lax.fori_loop(
        1, lax.axis_size(axis), lambda source, state: combine(state, take(source)), take(0)
    )


def rope_table(position, head_dim):
    half_width = head_dim // 2
    frequency = THETA ** (-(jnp.arange(half_width, dtype=jnp.float32) * 2.0 / head_dim))
    rotation = position.astype(jnp.float32)[:, None] * frequency[None, :]
    return (jnp.cos(rotation), jnp.sin(rotation))


def apply_rope(vectors, cosine, sine_table):
    half_width = vectors.shape[-1] // 2
    first_half = vectors[..., :half_width]
    second_half = vectors[..., half_width:]
    cos_rows = cosine[:, None, :]
    sin_rows = sine_table[:, None, :]
    return jnp.concatenate(
        [
            first_half * cos_rows - second_half * sin_rows,
            second_half * cos_rows + first_half * sin_rows,
        ],
        axis=-1,
    )


def merge_partials(earlier, later):
    top_early, total_early, accum_early = earlier
    top_late, total_late, accum_late = later
    highest = jnp.maximum(top_early, top_late)
    factor_early = jnp.exp(top_early - highest)
    factor_late = jnp.exp(top_late - highest)
    return (
        highest,
        total_early * factor_early + total_late * factor_late,
        accum_early * factor_early[..., None] + accum_late * factor_late[..., None],
    )


def softmax_terms(scores, valid_mask):
    masked = jnp.where(valid_mask, scores, NEG)
    highest = jnp.max(masked, axis=-1)
    weights = jnp.where(valid_mask, jnp.exp(masked - highest[..., None]), 0.0)
    return (highest, jnp.sum(weights, axis=-1), weights.astype(jnp.bfloat16))


def prompt_terms(queries, cache_block, lengths, first_place):
    head_dim = queries.shape[-1]
    keys_block = cache_block[..., :head_dim]
    values_block = cache_block[..., head_dim:]
    scores = jnp.einsum(
        "pntgqd,pgjd->pntgqj", queries, keys_block, preferred_element_type=jnp.float32
    ) * head_dim ** (-0.5)
    places = first_place + jnp.arange(cache_block.shape[2], dtype=jnp.int32)
    valid_mask = (places[None, :] < lengths[:, None])[:, None, None, None, None, :]
    highest, totals, weights = softmax_terms(scores, valid_mask)
    accum = jnp.einsum(
        "pntgqj,pgjd->pntgqd", weights, values_block, preferred_element_type=jnp.float32
    )
    return (highest, totals, accum)


def shards(
    hidden_in,
    attn_gain,
    mlp_gain,
    w_query,
    w_key,
    w_value,
    w_out,
    w_gate,
    w_up,
    w_down,
    prompt_cache,
    tail_cache,
    prompt_len,
    tail_len,
    prompt_of,
):
    model_index = lax.axis_index("mp")
    seq_index = lax.axis_index("seq")
    model_count = lax.axis_size("mp")
    seq_count = lax.axis_size("seq")
    row_total = hidden_in.shape[0]
    kv_local = prompt_cache.shape[1]
    local_span = prompt_cache.shape[2]
    head_local = w_query.shape[1] // HD
    req_local = tail_cache.shape[0]
    tail_span = tail_cache.shape[2]
    row_share = row_total // (model_count * seq_count)
    score_scale = HD ** (-0.5)
    wide_in = hidden_in.astype(jnp.float32)
    scaled_in = (wide_in * attn_gain.astype(jnp.float32)[None, :]).astype(jnp.bfloat16)
    query_part = jnp.dot(scaled_in, w_query, preferred_element_type=jnp.float32)
    key_part = jnp.dot(scaled_in, w_key, preferred_element_type=jnp.float32)
    value_part = jnp.dot(scaled_in, w_value, preferred_element_type=jnp.float32)
    square_part = jnp.sum(wide_in * wide_in, axis=1)
    query_sum, key_sum, value_sum, square_sum = lax.psum(
        (query_part, key_part, value_part, square_part), "mp"
    )
    input_rms = jnp.sqrt(square_sum / D)
    inverse_rms = lax.rsqrt(square_sum / D + EPS)
    prompt_match = prompt_of[:, None] == jnp.arange(PROMPTS, dtype=jnp.int32)[None, :]
    prompt_start = jnp.sum(jnp.where(prompt_match, prompt_len[None, :], 0), axis=1)
    position = (
        (prompt_start + tail_len)[:, None] + jnp.arange(2, dtype=jnp.int32)[None, :]
    ).reshape(row_total)
    cosine, sine_table = rope_table(position, HD)
    query = apply_rope(
        (query_sum * inverse_rms[:, None]).reshape(row_total, head_local, HD), cosine, sine_table
    ).astype(jnp.bfloat16)
    key_new = apply_rope(
        (key_sum * inverse_rms[:, None]).reshape(row_total, kv_local, HD), cosine, sine_table
    ).astype(jnp.bfloat16)
    value_new = (
        (value_sum * inverse_rms[:, None]).astype(jnp.bfloat16).reshape(row_total, kv_local, HD)
    )
    row_first = model_index * (2 * req_local)
    own_keys = lax.dynamic_slice_in_dim(key_new, row_first, 2 * req_local, 0)
    own_values = lax.dynamic_slice_in_dim(value_new, row_first, 2 * req_local, 0)
    entries = jnp.concatenate([own_keys, own_values], axis=-1).reshape(
        req_local, 2, kv_local, 2 * HD
    )
    new_entries = jnp.transpose(entries, (0, 2, 1, 3))
    order = jnp.argsort(prompt_of, stable=True)
    inverse_order = jnp.argsort(order)
    query_grid = query.reshape(REQ, 2, kv_local, QPK, HD)
    grouped = query_grid[order].reshape(PROMPTS, CONT, 2, kv_local, QPK, HD)
    first_place = model_index * local_span
    highest, totals, accum = prompt_terms(grouped, prompt_cache, prompt_len, first_place)
    prompt_top = highest.reshape(REQ, 2, head_local)[inverse_order].reshape(row_total, head_local)
    prompt_total = totals.reshape(REQ, 2, head_local)[inverse_order].reshape(row_total, head_local)
    prompt_accum = accum.reshape(REQ, 2, head_local, HD)[inverse_order].reshape(
        row_total, head_local, HD
    )
    own_query = lax.dynamic_slice_in_dim(query_grid, model_index * req_local, req_local, 0)
    own_tail = lax.dynamic_slice_in_dim(tail_len, model_index * req_local, req_local, 0)
    tail_scores = (
        jnp.einsum(
            "ntgqd,ngjd->ntgqj", own_query, tail_cache[..., :HD], preferred_element_type=jnp.float32
        )
        * score_scale
    )
    tail_mask = (jnp.arange(tail_span, dtype=jnp.int32)[None, :] < own_tail[:, None])[
        :, None, None, None, :
    ]
    tail_top, tail_total, tail_weights = softmax_terms(tail_scores, tail_mask)
    tail_accum = jnp.einsum(
        "ntgqj,ngjd->ntgqd", tail_weights, tail_cache[..., HD:], preferred_element_type=jnp.float32
    )
    self_keys = own_keys.reshape(req_local, 2, kv_local, HD)
    self_values = own_values.reshape(req_local, 2, kv_local, HD)
    self_scores = (
        jnp.einsum("ntgqd,nugd->ntgqu", own_query, self_keys, preferred_element_type=jnp.float32)
        * score_scale
    )
    step_mask = (
        jnp.arange(2, dtype=jnp.int32)[None, :] <= jnp.arange(2, dtype=jnp.int32)[:, None]
    )[None, :, None, None, :]
    self_top, self_total, self_weights = softmax_terms(self_scores, step_mask)
    self_accum = jnp.einsum(
        "ntgqu,nugd->ntgqd", self_weights, self_values, preferred_element_type=jnp.float32
    )
    own_top, own_total, own_accum = merge_partials(
        (tail_top, tail_total, tail_accum), (self_top, self_total, self_accum)
    )
    full_top = lax.dynamic_update_slice_in_dim(
        jnp.full((row_total, head_local), NEG, jnp.float32),
        own_top.reshape(2 * req_local, head_local),
        row_first,
        0,
    )
    full_total = lax.dynamic_update_slice_in_dim(
        jnp.zeros((row_total, head_local), jnp.float32),
        own_total.reshape(2 * req_local, head_local),
        row_first,
        0,
    )
    full_accum = lax.dynamic_update_slice_in_dim(
        jnp.zeros((row_total, head_local, HD), jnp.float32),
        own_accum.reshape(2 * req_local, head_local, HD),
        row_first,
        0,
    )
    local_top, local_total, local_accum = merge_partials(
        (prompt_top, prompt_total, prompt_accum), (full_top, full_total, full_accum)
    )
    merged_top, merged_total, merged_accum = joined(
        (local_top, local_total, local_accum), "mp", merge_partials
    )
    attention = (
        (merged_accum / merged_total[..., None])
        .astype(jnp.bfloat16)
        .reshape(row_total, head_local * HD)
    )
    max_logit = jnp.max(merged_top.reshape(REQ, 2, head_local), axis=1)
    head_part = jnp.dot(attention, w_out, preferred_element_type=jnp.float32)
    own_row = (model_index * seq_count + seq_index) * row_share
    head_whole = lax.psum(head_part, "seq")
    residual = (wide_in + head_whole).astype(jnp.bfloat16)
    piece = lax.all_gather(residual, "mp", axis=1, tiled=True)
    wide_piece = piece.astype(jnp.float32)
    gain_piece = mlp_gain.astype(jnp.float32)
    scaled_piece = (wide_piece * gain_piece[None, :]).astype(jnp.bfloat16)
    gate_acc = jnp.dot(scaled_piece, w_gate, preferred_element_type=jnp.float32)
    up_acc = jnp.dot(scaled_piece, w_up, preferred_element_type=jnp.float32)
    square_acc = jnp.sum(wide_piece * wide_piece, axis=1)
    own_piece = lax.dynamic_slice_in_dim(piece, own_row, row_share, 0)
    own_block = own_piece
    gate_acc, up_acc, square_acc, own_block = (gate_acc, up_acc, square_acc, own_block)
    inverse_mid = lax.rsqrt(square_acc / D + EPS)
    gate_value = gate_acc * inverse_mid[:, None]
    up_value = up_acc * inverse_mid[:, None]
    hidden = (jax.nn.silu(gate_value) * up_value).astype(jnp.bfloat16)
    mlp_rows = lax.psum_scatter(
        jnp.dot(hidden, w_down, preferred_element_type=jnp.float32),
        ("mp", "seq"),
        scatter_dimension=0,
        tiled=True,
    )
    layer_out = (own_block.astype(jnp.float32) + mlp_rows).astype(jnp.bfloat16)
    return (layer_out, input_rms, max_logit, new_entries)


def solution(mesh):
    in_specs = (
        P(None, "mp"),
        P("mp"),
        P(),
        P("mp", "seq"),
        P("mp", "seq"),
        P("mp", "seq"),
        P("seq", "mp"),
        P(None, ("mp", "seq")),
        P(None, ("mp", "seq")),
        P(("mp", "seq"), None),
        P(None, "seq", "mp", None),
        P("mp", "seq", None, None),
        P(),
        P(),
        P(),
    )
    out_specs = (P(("mp", "seq"), None), P(), P(None, "seq"), P("mp", "seq", None, None))
    return jax.shard_map(shards, mesh=mesh, in_specs=in_specs, out_specs=out_specs, check_vma=False)
```

profile of v0, /device:TPU:0, one launch (start us, length us, event | category | flops | bytes accessed | tf_op | source)
XLA Modules:
  0.0 821.1 jit_solution(7491996693346277574)
XLA Ops:
  7.3 0.8 convert_element_type.59
  8.0 4.9 fusion.84
  13.0 1.0 fusion.80
  14.0 1.0 fusion.82
  15.5 2.5 sort.34
  18.1 2.5 sort.35
  20.6 0.2 fusion.68
  20.8 24.3 %psum.36 = f32[256]{0:T(256)S(1)} all-reduce(f32[256]{0:T(256)S(1)} %fusion.68), channel_id=1, replica_groups=mesh['mp'=8,'seq'=4] {'mp'}, use_global_device_ids=true, to_apply=%region_2.0 | all-reduce | flops 256 | bytes 2048 | tf_op jit(solution)/shard_map/psum | solution.py:121
  45.1 0.6 multiply_sqrt_fusion
  45.8 0.5 multiply_cosine_fusion
  46.4 88.4 %all-reduce.6.cloned.1.call-done = (f32[256,2048]{1,0:T(8,128)}, f32[256,256]{1,0:T(8,128)}, f32[256,256]{1,0:T(8,128)}) async-done(((f32[256,2048]{1,0:T(8,128)}, f32[256,256]{1,0:T(8,128)}, f32[256,256]{1,0:T(8,128)}), (f32[256,2048]{1,0:T(8,128)}, f32[256,256]{1,0:T(8,128)}, f32[256,256]{1,0:T(8,128)})) %all-reduce.6.cloned.1.call-update) | async-done | bytes 2621456 | tf_op jit(solution)/shard_map/psum | solution.py:121
  134.9 1.1 multiply_convert_fusion
  136.1 0.3 fusion.107
  136.5 1.8 multiply_bitcast_fusion
  138.3 0.4 copy.141
  138.7 0.8 subtract_convert_fusion
  139.5 0.6 pad_maximum_fusion
  140.1 0.2 copy.128
  140.4 0.7 fusion.109
  141.2 0.7 slice-done.1
  141.9 1.3 fusion.108
  143.3 1.7 gather_fusion
  144.9 29.6 %bitcast_reduce_fusion = (f32[8,16,2,2,8]{4,2,1,3,0:T(2,128)S(1)}, f32[8,2,16,2,8,4096]{5,4,3,2,1,0:T(8,128)}) fusion(pred[8,4096]{1,0:T(8,128)(4,1)S(1)} %broadcast_compare_fusion, bf16[8,2,4096,256]{3,2,1,0:T(8,128)(2,1)} %param.27, bf16[8,16,2,2,8,128]{5,4,2,3,1,0:T(8,128)(2,1)} %bitcast.142), kind=kOutput, calls=%fused_computation.13 | convolution fusion | flops 4345294848 | bytes 84983808 | tf_op jit(solution)/shard_map/pntgqd,pgjd->pntgqj/dot_general | solution.py:74
  174.5 0.1 copy.95
  174.6 22.1 %fusion.6 = f32[8,16,2,2,8]{4,2,1,3,0:T(2,128)S(1)} fusion(f32[8,2,16,2,8,4096]{5,4,3,2,1,0:T(8,128)} %get-tuple-element.268, f32[8,16,2,2,8]{4,2,1,3,0:T(2,128)S(1)} %get-tuple-element.267, pred[8,4096]{1,0:T(8,128)(4,1)S(1)} %broadcast_compare_fusion), kind=kLoop, calls=%fused_computation.18 | loop fusion | flops 83881984 | bytes 67174400 | tf_op jit(solution)/shard_map/reduce_sum | solution.py:67
  196.8 30.3 %fusion.29 = f32[8,16,2,2,8,128]{5,4,2,1,3,0:T(8,128)} fusion(bf16[8,2,4096,256]{3,2,1,0:T(8,128)(2,1)} %param.27, f32[8,2,16,2,8,4096]{5,4,3,2,1,0:T(8,128)} %get-tuple-element.268, f32[8,16,2,2,8]{4,2,1,3,0:T(2,128)S(1)} %get-tuple-element.267, pred[8,4096]{1,0:T(8,128)(4,1)S(1)} %broadcast_compare_fusion), kind=kOutput, calls=%fused_computation.45 | convolution fusion | flops 4378853376 | bytes 86310912 | tf_op jit(solution)/shard_map/pntgqj,pgjd->pntgqd/dot_general | solution.py:80
  227.1 0.2 fusion.97
  227.3 0.4 fusion.75
  227.7 0.3 fusion.64
  228.0 2.9 fusion.61
  232.0 0.7 gather_fusion.2
  232.8 0.7 gather_fusion.1
  233.5 3.2 copy.107
  236.7 2.3 gather_fusion.3
  239.3 2.8 fusion.28
  242.2 35.5 %all-gather = f32[2048,16]{1,0:T(8,128)S(1)} all-gather(f32[256,16]{1,0:T(8,128)S(1)} %get-tuple-element.246), channel_id=2, replica_groups=mesh['mp'=8,'seq'=4] {'mp'}, dimensions={0}, use_global_device_ids=true | all-gather | bytes 147456 | tf_op jit(solution)/shard_map/all_gather | solution.py:18
  277.8 36.8 %all-gather.1 = f32[2048,16]{1,0:T(8,128)S(1)} all-gather(f32[256,16]{1,0:T(8,128)S(1)} %get-tuple-element.243), channel_id=3, replica_groups=mesh['mp'=8,'seq'=4] {'mp'}, dimensions={0}, use_global_device_ids=true | all-gather | bytes 147456 | tf_op jit(solution)/shard_map/all_gather | solution.py:18
  314.7 0.3 copy.115
  315.1 0.3 copy.116
  315.4 169.6 %all-gather.8.cloned.1.call-done = f32[2048,16,128]{2,1,0:T(8,128)} async-done(((f32[256,16,128]{2,1,0:T(8,128)}), f32[2048,16,128]{2,1,0:T(8,128)}) %all-gather.8.cloned.1.call-update) | async-done | bytes 16777232 | tf_op jit(solution)/shard_map/all_gather | solution.py:18
  484.9 1.7 slice.52
  486.7 28.6 %while.19 = (s32[]{:T(128)}, f32[256,16]{0,1:T(8,128)S(1)}, f32[256,16]{0,1:T(8,128)S(1)}, f32[256,16,128]{2,1,0:T(8,128)S(1)}, f32[8,256,16]{1,2,0:T(8,128)S(1)...) while((s32[]{:T(128)}, f32[256,16]{0,1:T(8,128)S(1)}, ...), condition=%wide.region_15.16_spmd, body=%wide.region_14.15_spmd.sunk | while | flops 1597445 | bytes 6520983 | solution.py:23
  486.9 3.8 fusion.120
  491.0 3.8 fusion.120
  495.1 3.8 fusion.120
  499.2 3.8 fusion.120
  503.3 3.8 fusion.120
  507.4 3.8 fusion.120
  511.5 3.8 fusion.120
  515.4 0.7 divide_convert_fusion
  516.2 4.5 fusion.70
  520.7 34.4 %all-reduce.4.cloned.1.call-done = f32[256,1024]{1,0:T(8,128)} async-done(((f32[256,1024]{1,0:T(8,128)}), f32[256,1024]{1,0:T(8,128)}) %all-reduce.4.cloned.1.call-update) | async-done | bytes 1048592 | tf_op jit(solution)/shard_map/psum | solution.py:222
  555.1 2.2 fusion.69
  557.4 73.8 %all-gather.6.cloned.1.call-done = bf16[256,8192]{1,0:T(8,128)(2,1)} async-done(((bf16[256,1024]{1,0:T(8,128)(2,1)}), bf16[256,8192]{1,0:T(8,128)(2,1)}) %all-gather.6.cloned.1.call-update) | async-done | bytes 4194320 | tf_op jit(solution)/shard_map/all_gather | solution.py:224
  631.2 3.3 fusion.17
  634.5 0.2 copy-done.3
  634.7 8.1 fusion.43
  642.8 22.7 %fusion.87 = f32[256,8192]{1,0:T(8,128)} fusion(bf16[896,8192]{1,0:T(8,128)(2,1)} %param.26, bf16[8192,896]{1,0:T(8,128)(2,1)} %param.25, bf16[256,8192]{1,0:T(8,128)(2,1)} %all-gather.6.cloned.1.call-done, f32[8192]{0:T(1024)S(1)} %convert_element_type.71, f32[256,896]{1,0:T(8,128)S(1)} %fusion.43, f32[256]{0:T(256)S(1)} %add_rsqrt_fusion), kind=kOutput, calls=%fused_computation.81 | convolution fusion | flops 7524089856 | bytes 42894336 | tf_op jit(solution)/shard_map/dot_general | solution.py:239
  665.5 0.7 copy-done.8
  666.3 0.6 copy.121
  667.1 0.2 reduce_max.45
  667.2 0.7 copy.120
  667.9 145.0 %reduce-scatter.2.cloned.1.call-done = f32[8,8192]{1,0:T(8,128)} async-done(((f32[256,8192]{1,0:T(8,128)}), f32[8,8192]{1,0:T(8,128)}) %reduce-scatter.2.cloned.1.call-update) | async-done | bytes 262160 | tf_op jit(solution)/shard_map/reduce_scatter | solution.py:238
  812.9 1.7 add_convert_fusion.1
  (115 shorter events, 4.6 us)
Async XLA Ops:
  7.2 5.8 copy-start
  7.2 5.8 copy-start.2
  7.2 6.8 copy-start.6
  7.2 127.7 %all-reduce.6.cloned.1.call-start = ((), (), s32[]{:S(2)}) async-start(), calls=%async_computation.5 | async-start | bytes 5242880 | tf_op jit(solution)/shard_map/psum | solution.py:121
  12.9 2.2 copy-start.12
  13.0 2.2 copy-start.14
  13.0 2.3 copy-start.13
  15.1 469.9 %all-gather.8.cloned.1.call-start = ((), (), s32[]{:S(2)}) async-start(), calls=%async_computation.4 | async-start | bytes 18874368 | tf_op jit(solution)/shard_map/all_gather | solution.py:18
  138.3 2.9 slice-start
  138.7 3.2 slice-start.1
  140.4 0.7 copy-start.7
  227.1 3.9 copy-start.9
  242.2 312.9 %all-reduce.4.cloned.1.call-start = ((), (), s32[]{:S(2)}) async-start(), calls=%async_computation.1 | async-start | bytes 2097152 | tf_op jit(solution)/shard_map/psum | solution.py:222
  515.3 5.3 copy-start.4
  516.2 41.2 %copy-start.11 = (bf16[8192]{0:T(1024)(128)(2,1)S(1)}, bf16[8192]{0:T(1024)(128)(2,1)}, u32[]{:S(2)}) copy-start(bf16[8192]{0:T(1024)(128)(2,1)} %param.19) | copy-start | bytes 49156
  520.7 110.6 %all-gather.6.cloned.1.call-start = ((), (), s32[]{:S(2)}) async-start(), calls=%async_computation.2 | async-start | bytes 4718592 | tf_op jit(solution)/shard_map/all_gather | solution.py:224
  557.3 255.6 %reduce-scatter.2.cloned.1.call-start = ((), (), s32[]{:S(2)}) async-start(), calls=%async_computation.3 | async-start | bytes 8650752 | tf_op jit(solution)/shard_map/reduce_scatter | solution.py:238
  631.2 3.4 copy-start.3
  665.5 149.1 %copy-start.1 = (bf16[1024,256]{1,0:T(8,128)(2,1)S(1)}, bf16[1024,256]{1,0:T(8,128)(2,1)}, u32[]{:S(2)}) copy-start(bf16[1024,256]{1,0:T(8,128)(2,1)} %param.22) | copy-start | bytes 1572868
  665.5 0.8 copy-start.8
  665.5 0.8 copy-start.10
  665.5 1.5 copy-start.5
Sparse Core Ops, SparseCore 0:
  15.2 119.6 all-reduce.5
  242.3 242.5 all-gather.7
  520.8 34.2 all-reduce.3
  557.5 73.7 all-gather.5
  665.6 147.2 reduce-scatter.1
where the time goes:
time: 822 us; the launch traced here: 821 us
  waiting for transfers between devices  511 us (62%)
  matrix products  107 us (13%)
  blocking collectives  96.6 us (12%)
  other arithmetic  72.6 us (9%)
  local copies, waits for them, and re-layouts  18.4 us (2%)
  between operations  14.3 us (2%)
    all_gather x1, waiting for transfers between devices, joined(): gathered = jax.tree.map(lambda a: lax.all_gather(a, axis), part)  170 us
    reduce_scatter x1, waiting for transfers between devices, shards(): lax.psum_scatter(jnp.dot(hidden, w_down, preferred_element_type=jnp.float...  145 us
    psum x1, waiting for transfers between devices, shards(): lax.psum((query_part, key_part, value_part, square_part), 'mp')  88.4 us
    all_gather x1, waiting for transfers between devices, shards(): piece = lax.all_gather(residual, 'mp', axis=1, tiled=True)  73.8 us
    all_gather x2, blocking collectives, joined(): gathered = jax.tree.map(lambda a: lax.all_gather(a, axis), part)  72.4 us
    psum x1, waiting for transfers between devices, shards(): head_whole = lax.psum(head_part, 'seq')  34.4 us
    dot_general x1, matrix products, prompt_terms(): jnp.einsum('pntgqj,pgjd->pntgqd', weights, values_block, preferred_elemen...  30.3 us
    add x8, other arithmetic, merge_partials(): accum_early * factor_early[..., None] + accum_late * factor_late[..., None]  29.7 us
  transfers between devices with their start and end apart: 5, of which 5 were waited for; matrix products, arithmetic and copies ran while one was open for 1% of the time, Pallas kernels for 0%

commit v1 on v0

--- a/solution.py
+++ b/solution.py
@@ -221,7 +221,12 @@
     own_row = (model_index * seq_count + seq_index) * row_share
     head_whole = lax.psum(head_part, "seq")
     residual = (wide_in + head_whole).astype(jnp.bfloat16)
-    piece = lax.all_gather(residual, "mp", axis=1, tiled=True)
+    ring = [residual]
+    for hop in range(7):
+        ring.append(lax.ppermute(ring[-1], "mp", [(dev, (dev + 1) % 8) for dev in range(8)]))
+    piece = jnp.roll(
+        jnp.concatenate(ring[::-1], axis=1), (lax.axis_index("mp") + 1) * ring[0].shape[1], axis=1
+    )
     wide_piece = piece.astype(jnp.float32)
     gain_piece = mlp_gain.astype(jnp.float32)
     scaled_piece = (wide_piece * gain_piece[None, :]).astype(jnp.bfloat16)

time: 822 us -> 844 us (1.027)
  waiting for transfers between devices: 511 us -> 529 us
    ppermute x0 -> x7, waiting for transfers between devices: none -> 94.7 us  [shards(): lax.ppermute(ring[-1], 'mp', [(dev, (dev + 1) % 8) for dev in range(8)])]
    all_gather x1 -> x0, waiting for transfers between devices: 73.8 us -> none  [shards(): piece = lax.all_gather(residual, 'mp', axis=1, tiled=True)]
    dot_general x1, matrix products: 22.7 us -> 12 us  [shards(): jnp.dot(hidden, w_down, preferred_element_type=jnp.float32)]
  transfers between devices with their start and end apart: 5 -> 11, of which waited for: 5 -> 11; matrix products, arithmetic and copies ran while one was open for 1% -> 1% of each run, Pallas kernels for 0% -> 0%
where the time goes in v1:
time: 844 us; the launch traced here: 843 us
  waiting for transfers between devices  529 us (63%)
  matrix products  106 us (13%)
  blocking collectives  98.4 us (12%)
  other arithmetic  69.6 us (8%)
  local copies, waits for them, and re-layouts  23.2 us (3%)
  between operations  14.5 us (2%)
    all_gather x1, waiting for transfers between devices, joined(): gathered = jax.tree.map(lambda a: lax.all_gather(a, axis), part)  168 us
    reduce_scatter x1, waiting for transfers between devices, shards(): lax.psum_scatter(jnp.dot(hidden, w_down, preferred_element_type=jnp.float...  144 us
    ppermute x7, waiting for transfers between devices, shards(): lax.ppermute(ring[-1], 'mp', [(dev, (dev + 1) % 8) for dev in range(8)])  94.7 us
    psum x1, waiting for transfers between devices, shards(): lax.psum((query_part, key_part, value_part, square_part), 'mp')  88.4 us
    all_gather x2, blocking collectives, joined(): gathered = jax.tree.map(lambda a: lax.all_gather(a, axis), part)  74.2 us
    psum x1, waiting for transfers between devices, shards(): head_whole = lax.psum(head_part, 'seq')  34.4 us
    dot_general x1, matrix products, prompt_terms(): jnp.einsum('pntgqj,pgjd->pntgqd', weights, values_block, preferred_elemen...  30.3 us
    add x8, other arithmetic, merge_partials(): accum_early * factor_early[..., None] + accum_late * factor_late[..., None]  29.7 us
  transfers between devices with their start and end apart: 11, of which 11 were waited for; matrix products, arithmetic and copies ran while one was open for 1% of the time, Pallas kernels for 0%

profile of v1, /device:TPU:0, one launch (start us, length us, event | category | flops | bytes accessed | tf_op | source)
XLA Modules:
  0.0 843.2 jit_solution(5780547213810019288)
XLA Ops:
  7.3 0.8 convert_element_type.59
  8.1 4.9 fusion.80
  13.0 2.1 fusion.76
  15.0 2.2 fusion.78
  17.8 2.5 sort.34
  20.3 2.5 sort.35
  23.0 24.3 %psum.36 = f32[256]{0:T(256)S(1)} all-reduce(f32[256]{0:T(256)S(1)} %fusion.62), channel_id=1, replica_groups=mesh['mp'=8,'seq'=4] {'mp'}, use_global_device_ids=true, to_apply=%region_2.0 | all-reduce | flops 256 | bytes 2048 | tf_op jit(solution)/shard_map/psum | solution.py:121
  47.4 0.6 multiply_sqrt_fusion
  48.0 0.5 multiply_cosine_fusion
  48.6 88.4 %all-reduce.6.cloned.1.call-done = (f32[256,2048]{1,0:T(8,128)}, f32[256,256]{1,0:T(8,128)}, f32[256,256]{1,0:T(8,128)}) async-done(((f32[256,2048]{1,0:T(8,128)}, f32[256,256]{1,0:T(8,128)}, f32[256,256]{1,0:T(8,128)}), (f32[256,2048]{1,0:T(8,128)}, f32[256,256]{1,0:T(8,128)}, f32[256,256]{1,0:T(8,128)})) %all-reduce.6.cloned.1.call-update) | async-done | bytes 2621456 | tf_op jit(solution)/shard_map/psum | solution.py:121
  137.1 1.1 multiply_convert_fusion.2
  138.7 1.8 multiply_bitcast_fusion
  140.9 0.8 subtract_convert_fusion
  141.7 0.6 pad_maximum_fusion
  142.6 0.7 fusion.104
  143.4 0.7 slice-done.1
  144.1 1.3 fusion.103
  145.5 1.7 gather_fusion
  147.1 29.6 %bitcast_reduce_fusion = (f32[8,16,2,2,8]{4,2,1,3,0:T(2,128)S(1)}, f32[8,2,16,2,8,4096]{5,4,3,2,1,0:T(8,128)}) fusion(pred[8,4096]{1,0:T(8,128)(4,1)S(1)} %broadcast_compare_fusion, bf16[8,2,4096,256]{3,2,1,0:T(8,128)(2,1)} %param.27, bf16[8,16,2,2,8,128]{5,4,2,3,1,0:T(8,128)(2,1)} %bitcast.142), kind=kOutput, calls=%fused_computation.13 | convolution fusion | flops 4345294848 | bytes 84983808 | tf_op jit(solution)/shard_map/pntgqd,pgjd->pntgqj/dot_general | solution.py:74
  176.9 22.1 %fusion.6 = f32[8,16,2,2,8]{4,2,1,3,0:T(2,128)S(1)} fusion(f32[8,2,16,2,8,4096]{5,4,3,2,1,0:T(8,128)} %get-tuple-element.268, f32[8,16,2,2,8]{4,2,1,3,0:T(2,128)S(1)} %get-tuple-element.267, pred[8,4096]{1,0:T(8,128)(4,1)S(1)} %broadcast_compare_fusion), kind=kLoop, calls=%fused_computation.18 | loop fusion | flops 83881984 | bytes 67174400 | tf_op jit(solution)/shard_map/reduce_sum | solution.py:67
  199.0 30.3 %fusion.29 = f32[8,16,2,2,8,128]{5,4,2,1,3,0:T(8,128)} fusion(bf16[8,2,4096,256]{3,2,1,0:T(8,128)(2,1)} %param.27, f32[8,2,16,2,8,4096]{5,4,3,2,1,0:T(8,128)} %get-tuple-element.268, f32[8,16,2,2,8]{4,2,1,3,0:T(2,128)S(1)} %get-tuple-element.267, pred[8,4096]{1,0:T(8,128)(4,1)S(1)} %broadcast_compare_fusion), kind=kOutput, calls=%fused_computation.45 | convolution fusion | flops 4378853376 | bytes 86310912 | tf_op jit(solution)/shard_map/pntgqj,pgjd->pntgqd/dot_general | solution.py:80
  230.2 2.9 fusion.55
  234.2 0.7 gather_fusion.2
  234.9 0.7 gather_fusion.1
  235.7 3.2 copy.107
  238.9 2.3 gather_fusion.3
  241.5 2.8 fusion.28
  244.4 35.5 %all-gather = f32[2048,16]{1,0:T(8,128)S(1)} all-gather(f32[256,16]{1,0:T(8,128)S(1)} %get-tuple-element.246), channel_id=2, replica_groups=mesh['mp'=8,'seq'=4] {'mp'}, dimensions={0}, use_global_device_ids=true | all-gather | bytes 147456 | tf_op jit(solution)/shard_map/all_gather | solution.py:18
  280.0 38.6 %all-gather.1 = f32[2048,16]{1,0:T(8,128)S(1)} all-gather(f32[256,16]{1,0:T(8,128)S(1)} %get-tuple-element.243), channel_id=3, replica_groups=mesh['mp'=8,'seq'=4] {'mp'}, dimensions={0}, use_global_device_ids=true | all-gather | bytes 147456 | tf_op jit(solution)/shard_map/all_gather | solution.py:18
  319.3 167.7 %all-gather.5.cloned.1.call-done = f32[2048,16,128]{2,1,0:T(8,128)} async-done(((f32[256,16,128]{2,1,0:T(8,128)}), f32[2048,16,128]{2,1,0:T(8,128)}) %all-gather.5.cloned.1.call-update) | async-done | bytes 16777232 | tf_op jit(solution)/shard_map/all_gather | solution.py:18
  487.0 1.7 slice.52
  488.7 28.6 %while.19 = (s32[]{:T(128)}, f32[256,16]{0,1:T(8,128)S(1)}, f32[256,16]{0,1:T(8,128)S(1)}, f32[256,16,128]{2,1,0:T(8,128)S(1)}, f32[8,256,16]{1,2,0:T(8,128)S(1)...) while((s32[]{:T(128)}, f32[256,16]{0,1:T(8,128)S(1)}, ...), condition=%wide.region_15.16_spmd, body=%wide.region_14.15_spmd.sunk | while | flops 1597445 | bytes 6520983 | solution.py:23
  489.0 3.8 fusion.115
  493.1 3.8 fusion.115
  497.2 3.8 fusion.115
  501.3 3.8 fusion.115
  505.3 3.8 fusion.115
  509.4 3.8 fusion.115
  513.5 3.8 fusion.115
  517.5 0.7 divide_convert_fusion
  518.2 4.5 fusion.64
  522.8 34.4 %all-reduce.4.cloned.1.call-done = f32[256,1024]{1,0:T(8,128)} async-done(((f32[256,1024]{1,0:T(8,128)}), f32[256,1024]{1,0:T(8,128)}) %all-reduce.4.cloned.1.call-update) | async-done | bytes 1048592 | tf_op jit(solution)/shard_map/psum | solution.py:222
  557.2 1.4 fusion.63
  558.5 1.5 collective-permute-start
  560.1 14.7 %collective-permute-done = bf16[256,1024]{1,0:T(8,128)(2,1)S(1)} collective-permute-done((bf16[256,1024]{1,0:T(8,128)(2,1)S(1)}, bf16[256,1024]{1,0:T(8,128)(2,1)S(1)}, u32[]{:S(2)}, u32[]{:S(2)}) %collective-permute-start) | collective-permute-done | bytes 524320 | tf_op jit(solution)/shard_map/ppermute | solution.py:226
  574.7 15.2 %collective-permute-done.1 = bf16[256,1024]{1,0:T(8,128)(2,1)S(1)} collective-permute-done((bf16[256,1024]{1,0:T(8,128)(2,1)S(1)}, bf16[256,1024]{1,0:T(8,128)(2,1)S(1)}, u32[]{:S(2)}, u32[]{:S(2)}) %collective-permute-start.1) | collective-permute-done | bytes 524320 | tf_op jit(solution)/shard_map/ppermute | solution.py:226
  590.0 14.3 %collective-permute-done.2 = bf16[256,1024]{1,0:T(8,128)(2,1)S(1)} collective-permute-done((bf16[256,1024]{1,0:T(8,128)(2,1)S(1)}, bf16[256,1024]{1,0:T(8,128)(2,1)S(1)}, u32[]{:S(2)}, u32[]{:S(2)}) %collective-permute-start.2) | collective-permute-done | bytes 524320 | tf_op jit(solution)/shard_map/ppermute | solution.py:226
  604.3 13.4 %collective-permute-done.3 = bf16[256,1024]{1,0:T(8,128)(2,1)S(1)} collective-permute-done((bf16[256,1024]{1,0:T(8,128)(2,1)S(1)}, bf16[256,1024]{1,0:T(8,128)(2,1)S(1)}, u32[]{:S(2)}, u32[]{:S(2)}) %collective-permute-start.3) | collective-permute-done | bytes 524320 | tf_op jit(solution)/shard_map/ppermute | solution.py:226
  617.7 12.5 %collective-permute-done.4 = bf16[256,1024]{1,0:T(8,128)(2,1)S(1)} collective-permute-done((bf16[256,1024]{1,0:T(8,128)(2,1)S(1)}, bf16[256,1024]{1,0:T(8,128)(2,1)S(1)}, u32[]{:S(2)}, u32[]{:S(2)}) %collective-permute-start.4) | collective-permute-done | bytes 524320 | tf_op jit(solution)/shard_map/ppermute | solution.py:226
  630.2 12.4 %collective-permute-done.5 = bf16[256,1024]{1,0:T(8,128)(2,1)} collective-permute-done((bf16[256,1024]{1,0:T(8,128)(2,1)S(1)}, bf16[256,1024]{1,0:T(8,128)(2,1)}, u32[]{:S(2)}, u32[]{:S(2)}) %collective-permute-start.5) | collective-permute-done | bytes 524320 | tf_op jit(solution)/shard_map/ppermute | solution.py:226
  642.6 12.2 %collective-permute-done.6 = bf16[256,1024]{1,0:T(8,128)(2,1)} collective-permute-done((bf16[256,1024]{1,0:T(8,128)(2,1)}, bf16[256,1024]{1,0:T(8,128)(2,1)}, u32[]{:S(2)}, u32[]{:S(2)}) %collective-permute-start.6) | collective-permute-done | bytes 524320 | tf_op jit(solution)/shard_map/ppermute | solution.py:226
  654.8 1.1 constant_dynamic-update-slice_fusion.15
  655.9 1.1 constant_dynamic-update-slice_fusion.14
  657.2 1.1 constant_dynamic-update-slice_fusion.7
  658.3 1.1 constant_dynamic-update-slice_fusion.6
  659.7 0.9 fusion.17
  660.6 11.1 %fusion.43 = f32[256,896]{1,0:T(8,128)S(1)} fusion(bf16[8192,896]{1,0:T(8,128)(2,1)} %param.24, f32[8192]{0:T(1024)S(1)} %convert_element_type.71, bf16[256,16384]{1,0:T(8,128)(2,1)S(1)} %constant_dynamic-update-slice_fusion, s32[]{:T(128)S(6)} %select_n.103, f32[256]{0:T(256)S(1)} %add_rsqrt_fusion), kind=kOutput, calls=%fused_computation.52 | convolution fusion | flops 3764617216 | bytes 19825668 | tf_op jit(solution)/shard_map/dot_general | solution.py:233
  672.1 4.5 fusion.46
  676.6 12.0 %fusion.74 = f32[256,8192]{1,0:T(8,128)} fusion(bf16[896,8192]{1,0:T(8,128)(2,1)} %param.26, f32[256,896]{1,0:T(8,128)S(1)} %fusion.46, f32[256,896]{1,0:T(8,128)S(1)} %fusion.43), kind=kOutput, calls=%fused_computation.77 | convolution fusion | flops 3759472640 | bytes 24903680 | tf_op jit(solution)/shard_map/dot_general | solution.py:244
  688.7 0.7 copy-done.5
  689.4 0.6 copy.121
  690.3 0.7 copy.120
  691.0 143.9 %reduce-scatter.2.cloned.1.call-done = f32[8,8192]{1,0:T(8,128)} async-done(((f32[256,8192]{1,0:T(8,128)}), f32[8,8192]{1,0:T(8,128)}) %reduce-scatter.2.cloned.1.call-update) | async-done | bytes 262160 | tf_op jit(solution)/shard_map/reduce_scatter | solution.py:243
  834.8 1.8 add_convert_fusion.1
  (142 shorter events, 8.1 us)
Async XLA Ops:
  7.2 5.8 copy-start
  7.2 15.7 %copy-start.2 = (bf16[256,1024]{1,0:T(8,128)(2,1)S(1)}, bf16[256,1024]{1,0:T(8,128)(2,1)}, u32[]{:S(2)}) copy-start(bf16[256,1024]{1,0:T(8,128)(2,1)} %param.17) | copy-start | bytes 1572868
  7.2 10.1 %copy-start.7 = (s32[8]{0:T(128)S(1)}, s32[8]{0:T(128)}, u32[]{:S(2)}) copy-start(s32[8]{0:T(128)} %param.29) | copy-start | bytes 100
  7.2 10.1 %copy-start.9 = (s32[128]{0:T(128)S(1)}, s32[128]{0:T(128)}, u32[]{:S(2)}) copy-start(s32[128]{0:T(128)} %param.31) | copy-start | bytes 1540
  7.2 10.2 %copy-start.8 = (s32[128]{0:T(128)S(1)}, s32[128]{0:T(128)}, u32[]{:S(2)}) copy-start(s32[128]{0:T(128)} %param.30) | copy-start | bytes 1540
  7.2 129.9 %all-reduce.6.cloned.1.call-start = ((), (), s32[]{:S(2)}) async-start(), calls=%async_computation.4 | async-start | bytes 5242880 | tf_op jit(solution)/shard_map/psum | solution.py:121
  17.3 469.7 %all-gather.5.cloned.1.call-start = ((), (), s32[]{:S(2)}) async-start(), calls=%async_computation.3 | async-start | bytes 18874368 | tf_op jit(solution)/shard_map/all_gather | solution.py:18
  140.5 2.9 slice-start
  140.9 3.2 slice-start.1
  142.6 0.7 copy-start.4
  244.4 312.8 %all-reduce.4.cloned.1.call-start = ((), (), s32[]{:S(2)}) async-start(), calls=%async_computation.1 | async-start | bytes 2097152 | tf_op jit(solution)/shard_map/psum | solution.py:222
  517.4 125.2 %copy-start.6 = (bf16[8192]{0:T(1024)(128)(2,1)S(1)}, bf16[8192]{0:T(1024)(128)(2,1)}, u32[]{:S(2)}) copy-start(bf16[8192]{0:T(1024)(128)(2,1)} %param.19) | copy-start | bytes 49156
  522.7 312.1 %reduce-scatter.2.cloned.1.call-start = ((), (), s32[]{:S(2)}) async-start(), calls=%async_computation.2 | async-start | bytes 8650752 | tf_op jit(solution)/shard_map/reduce_scatter | solution.py:243
  558.5 16.2 %collective-permute-start = (bf16[256,1024]{1,0:T(8,128)(2,1)S(1)}, bf16[256,1024]{1,0:T(8,128)(2,1)S(1)}, u32[]{:S(2)}, u32[]{:S(2)}) collective-permute-start(bf16[256,1024]{1,0:T(8,128)(2,1)S(1)} %fusion.63), channel_id=1, source_target_pairs={{0,4},{4,8},{8,12},{12,16},{16,20},{20,24},{24,28},{28,0},{1,5},{5... | collective-permute-start | bytes 1572872 | tf_op jit(solution)/shard_map/ppermute | solution.py:226
  574.7 15.2 %collective-permute-start.1 = (bf16[256,1024]{1,0:T(8,128)(2,1)S(1)}, bf16[256,1024]{1,0:T(8,128)(2,1)S(1)}, u32[]{:S(2)}, u32[]{:S(2)}) collective-permute-start(bf16[256,1024]{1,0:T(8,128)(2,1)S(1)} %collective-permute-done), channel_id=1, source_target_pairs={{0,4},{4,8},{8,12},{12,16},{16,20},{20,24},{24,28},{28,0},{1,5},{5... | collective-permute-start | bytes 1572872 | tf_op jit(solution)/shard_map/ppermute | solution.py:226
  590.0 14.3 %collective-permute-start.2 = (bf16[256,1024]{1,0:T(8,128)(2,1)S(1)}, bf16[256,1024]{1,0:T(8,128)(2,1)S(1)}, u32[]{:S(2)}, u32[]{:S(2)}) collective-permute-start(bf16[256,1024]{1,0:T(8,128)(2,1)S(1)} %collective-permute-done.1), channel_id=1, source_target_pairs={{0,4},{4,8},{8,12},{12,16},{16,20},{20,24},{24,28},{28,0},{1,5},{5... | collective-permute-start | bytes 1572872 | tf_op jit(solution)/shard_map/ppermute | solution.py:226
  604.3 13.4 %collective-permute-start.3 = (bf16[256,1024]{1,0:T(8,128)(2,1)S(1)}, bf16[256,1024]{1,0:T(8,128)(2,1)S(1)}, u32[]{:S(2)}, u32[]{:S(2)}) collective-permute-start(bf16[256,1024]{1,0:T(8,128)(2,1)S(1)} %collective-permute-done.2), channel_id=1, source_target_pairs={{0,4},{4,8},{8,12},{12,16},{16,20},{20,24},{24,28},{28,0},{1,5},{5... | collective-permute-start | bytes 1572872 | tf_op jit(solution)/shard_map/ppermute | solution.py:226
  617.7 12.5 %collective-permute-start.4 = (bf16[256,1024]{1,0:T(8,128)(2,1)S(1)}, bf16[256,1024]{1,0:T(8,128)(2,1)S(1)}, u32[]{:S(2)}, u32[]{:S(2)}) collective-permute-start(bf16[256,1024]{1,0:T(8,128)(2,1)S(1)} %collective-permute-done.3), channel_id=1, source_target_pairs={{0,4},{4,8},{8,12},{12,16},{16,20},{20,24},{24,28},{28,0},{1,5},{5... | collective-permute-start | bytes 1572872 | tf_op jit(solution)/shard_map/ppermute | solution.py:226
  630.2 12.4 %collective-permute-start.5 = (bf16[256,1024]{1,0:T(8,128)(2,1)S(1)}, bf16[256,1024]{1,0:T(8,128)(2,1)}, u32[]{:S(2)}, u32[]{:S(2)}) collective-permute-start(bf16[256,1024]{1,0:T(8,128)(2,1)S(1)} %collective-permute-done.4), channel_id=1, source_target_pairs={{0,4},{4,8},{8,12},{12,16},{16,20},{20,24},{24,28},{28,0},{1,5},{5... | collective-permute-start | bytes 1572872 | tf_op jit(solution)/shard_map/ppermute | solution.py:226
  642.6 12.2 %collective-permute-start.6 = (bf16[256,1024]{1,0:T(8,128)(2,1)}, bf16[256,1024]{1,0:T(8,128)(2,1)}, u32[]{:S(2)}, u32[]{:S(2)}) collective-permute-start(bf16[256,1024]{1,0:T(8,128)(2,1)} %collective-permute-done.5), channel_id=1, source_target_pairs={{0,4},{4,8},{8,12},{12,16},{16,20},{20,24},{24,28},{28,0},{1,5},{5... | collective-permute-start | bytes 1572872 | tf_op jit(solution)/shard_map/ppermute | solution.py:226
  659.6 12.2 %slice-start.2 = ((s8[14680064]{0:T(1024)(128)(4,1)}), s8[4194304]{0:T(1024)(128)(4,1)S(1)}, s32[]{:S(2)}) async-start(s8[14680064]{0:T(1024)(128)(4,1)} %bitcast.153), calls=%async_computation.7 | async-start | bytes 8388608
  659.7 12.1 %copy-start.3 = (bf16[256,16384]{1,0:T(8,128)(2,1)}, bf16[256,16384]{1,0:T(8,128)(2,1)S(1)}, u32[]{:S(2)}) copy-start(bf16[256,16384]{1,0:T(8,128)(2,1)S(1)} %constant_dynamic-update-slice_fusion) | copy-start | bytes 25165828
  660.6 11.2 %slice-start.3 = ((s8[14680064]{0:T(1024)(128)(4,1)}), s8[4194304]{0:T(1024)(128)(4,1)S(1)}, s32[]{:S(2)}) async-start(s8[14680064]{0:T(1024)(128)(4,1)} %bitcast.153), calls=%async_computation.8 | async-start | bytes 8388608
  660.6 11.2 %slice-start.4 = ((s8[14680064]{0:T(1024)(128)(4,1)}), s8[4194304]{0:T(1024)(128)(4,1)S(1)}, s32[]{:S(2)}) async-start(s8[14680064]{0:T(1024)(128)(4,1)} %bitcast.153), calls=%async_computation.9 | async-start | bytes 8388608
  660.6 11.4 %slice-start.5 = ((s8[14680064]{0:T(1024)(128)(4,1)}), s8[2097152]{0:T(1024)(128)(4,1)S(1)}, s32[]{:S(2)}) async-start(s8[14680064]{0:T(1024)(128)(4,1)} %bitcast.153), calls=%async_computation.10 | async-start | bytes 4194304
  676.6 160.0 %copy-start.1 = (bf16[1024,256]{1,0:T(8,128)(2,1)S(1)}, bf16[1024,256]{1,0:T(8,128)(2,1)}, u32[]{:S(2)}) copy-start(bf16[1024,256]{1,0:T(8,128)(2,1)} %param.22) | copy-start | bytes 1572868
  688.6 0.7 copy-start.5
Sparse Core Ops, SparseCore 0:
  17.4 119.6 all-reduce.5
  244.5 242.4 all-gather.4
  522.8 34.2 all-reduce.3
  688.8 146.0 reduce-scatter.1
